TPU v7x, 32 devices: a whole 2x2x4 slice. The times are simulated.
32 devices in a mesh: runs: 2 (over x), tm: 8 (over z, y), hyd: 2 (over core).
Axes of the slice: x: 2, y: 2, z: 4, core: 2. Of those that a mesh axis runs over, the one named last changes fastest.
Arguments:
- record: bfloat16 [524160, 1024], P(('runs', 'tm'), 'hyd'), parts along dimension 0, may hold values from -6 to 6
- chips: int32 [4095], replicated, may hold values from -1 to 1, as said below
- steer_lags: int32 [1024, 256], P('hyd'), may hold values from 0 to 7
Outputs:
- power: float32 [128, 512, 256], P('runs', 'tm', 'hyd'), parts along dimension 0
There are 2 independent parts, one for each index of `runs`. A program takes and returns all parts, laid end to end along the dimension named above; an argument that names none is the same for every part. Nothing has to cross between parts.
Inputs may be any that keep to these rules, and one draw needn't show every extreme that they name: The chips are +1 or -1 and form one period of a maximal-length sequence of period 4095, starting at a drawn phase.
All inputs are finite; a program needn't handle non-finite values.
Results may differ from a plain program's by a relative error of at most 0.0047.
Values may be sent and summed in bfloat16 or wider, within the bound.
A program may use at most 256 MiB of HBM per device.

v0:
```python
import math
import jax
import jax.numpy as jnp
from jax import lax
from jax.sharding import PartitionSpec as P

CODE = 4095
HYDRO = 1024
DELAYS = 512
PERIODS = 64
BEAMS = 256
MAXLAG = 8


def passed_along(array, axis, by):
    length = lax.axis_size(axis)
    pairs = [(i, i + by) for i in range(length) if 0 <= i + by < length]
    return lax.ppermute(array, axis, pairs)


def toeplitz_code(chips):
    seg_len = CODE + DELAYS - 1
    padded = jnp.concatenate([chips.astype(jnp.float32), jnp.zeros((DELAYS,), jnp.float32)])
    tiled = jnp.tile(padded, DELAYS)[: DELAYS * seg_len]
    return tiled.reshape(DELAYS, seg_len).astype(jnp.bfloat16)


def dft_table(length):
    freq = jnp.arange(length, dtype=jnp.int32)
    phase = (freq[:, None] * freq[None, :] % length).astype(jnp.float32) * (2.0 * math.pi / length)
    weight = 1.0 / math.sqrt(length)
    return jnp.concatenate([jnp.cos(phase) * weight, -jnp.sin(phase) * weight], 0).astype(
        jnp.bfloat16
    )


def body(record, chips, steer_lags):
    hyd_local = record.shape[1]
    tm_size = lax.axis_size("tm")
    local_periods = PERIODS // tm_size
    delay_rows = DELAYS // tm_size
    seg_len = CODE + DELAYS - 1
    norm_code = 1.0 / math.sqrt(CODE)
    tail_rows = passed_along(record[: DELAYS - 1], "tm", -1)
    extended = jnp.concatenate([record, tail_rows], 0)
    toeplitz = toeplitz_code(chips)
    profile_list = []
    for period in range(local_periods):
        segment = extended[period * CODE : period * CODE + seg_len]
        profile_list.append(
            (jnp.dot(toeplitz, segment, preferred_element_type=jnp.float32) * norm_code).astype(
                jnp.bfloat16
            )
        )
    profiles = jnp.stack(profile_list, 0)
    transform = dft_table(PERIODS)
    received = lax.all_to_all(profiles, "tm", split_axis=1, concat_axis=0, tiled=True)
    trailing = received.shape[1:]
    flattened = received.reshape(received.shape[0], -1)
    spectral = jnp.dot(transform, flattened, preferred_element_type=jnp.float32).astype(
        jnp.bfloat16
    )
    spectrum = spectral.reshape((2, received.shape[0]) + trailing)
    next_rows = passed_along(spectrum[:, :, : MAXLAG - 1, :], "tm", -1)
    spec_ext = jnp.concatenate([spectrum, next_rows], 2)
    norm_hydro = 1.0 / math.sqrt(HYDRO)
    shifted_list = [
        spec_ext[:, :, offset : offset + delay_rows, :].reshape(2 * PERIODS * delay_rows, hyd_local)
        for offset in range(MAXLAG)
    ]
    beam_local = BEAMS // lax.axis_size("hyd")
    partial_sum = jnp.zeros((2 * PERIODS * delay_rows, BEAMS), jnp.float32)
    for offset in range(MAXLAG):
        selector = (steer_lags == offset).astype(jnp.bfloat16)
        partial_sum = partial_sum + jnp.dot(
            shifted_list[offset], selector, preferred_element_type=jnp.float32
        )
    summed = lax.psum(partial_sum * norm_hydro, "hyd")
    owned = lax.dynamic_slice_in_dim(summed, lax.axis_index("hyd") * beam_local, beam_local, 1)
    owned = owned.reshape(2, PERIODS, delay_rows, beam_local)
    return owned[0] * owned[0] + owned[1] * owned[1]


def solution(mesh):
    in_specs = (P(("runs", "tm"), "hyd"), P(), P("hyd", None))
    out_specs = P("runs", "tm", "hyd")
    return jax.shard_map(body, mesh=mesh, in_specs=in_specs, out_specs=out_specs, check_vma=False)
```

profile of v0, /device:TPU:0, one launch (start us, length us, event | category | flops | bytes accessed | tf_op | source)
XLA Modules:
  0.0 408.6 jit_solution(9783359401931948476)
XLA Ops:
  12.1 11.8 %tile.11 = bf16[2358784]{0:T(1024)(128)(2,1)} reshape(bf16[512,4607]{1,0:T(8,128)(2,1)} %tile.10) | data formatting | bytes 9435136 | tf_op jit(solution)/shard_map/tile | solution.py:24
  23.9 5.7 %slice.85 = bf16[2358272]{0:T(1024)(128)(2,1)} slice(bf16[2358784]{0:T(1024)(128)(2,1)} %tile.11), slice={[0:2358272]} | slice | bytes 9433088 | tf_op jit(solution)/shard_map/slice | solution.py:24
  29.6 11.3 %convert_element_type.50 = bf16[512,4606]{1,0:T(8,128)(2,1)} reshape(bf16[2358272]{0:T(1024)(128)(2,1)} %slice.85) | data formatting | bytes 9433088 | tf_op jit(solution)/shard_map/convert_element_type | solution.py:25
  40.9 7.3 %fusion.65 = bf16[8,512,512]{2,1,0:T(8,128)(2,1)} fusion(bf16[512,4606]{1,0:T(8,128)(2,1)} %convert_element_type.50, bf16[32760,512]{1,0:T(8,128)(2,1)} %param.3), kind=kOutput, calls=%fused_computation.47 | convolution fusion | flops 2415394816 | bytes 9961472 | tf_op jit(solution)/shard_map/dot_general | solution.py:51
  48.3 5.9 %fusion.73 = bf16[8,512,512]{2,1,0:T(8,128)(2,1)} fusion(bf16[8,512,512]{2,1,0:T(8,128)(2,1)} %fusion.65, bf16[512,4606]{1,0:T(8,128)(2,1)S(1)} %copy-done.1, bf16[32760,512]{1,0:T(8,128)(2,1)} %param.3), kind=kOutput, calls=%fused_computation.51 | convolution fusion | flops 2415394816 | bytes 9959424 | tf_op jit(solution)/shard_map/dot_general | solution.py:51
  54.2 6.6 %fusion.79 = bf16[8,512,512]{2,1,0:T(8,128)(2,1)} fusion(bf16[8,512,512]{2,1,0:T(8,128)(2,1)} %fusion.73, bf16[512,4606]{1,0:T(8,128)(2,1)S(1)} %copy-done.1, bf16[32760,512]{1,0:T(8,128)(2,1)} %param.3), kind=kOutput, calls=%fused_computation.53 | convolution fusion | flops 2415394816 | bytes 9959424 | tf_op jit(solution)/shard_map/dot_general | solution.py:51
  76.5 5.9 %fusion.69 = bf16[8,512,512]{2,1,0:T(8,128)(2,1)} fusion(bf16[8,512,512]{2,1,0:T(8,128)(2,1)} %fusion.103, bf16[512,4606]{1,0:T(8,128)(2,1)} %convert_element_type.50, bf16[511,512]{1,0:T(8,128)(2,1)S(1)} %collective-permute-done, bf16[32760,512]{1,0:T(8,128)(2,1)S(1)} %bitcast.82), kind=kOutput, calls=%fused_computation.49 | convolution fusion | flops 2424827904 | bytes 39312384 | tf_op jit(solution)/shard_map/dot_general | solution.py:51
  82.5 6.9 %copy.5 = bf16[8,512,512]{2,0,1:T(8,128)(2,1)} copy(bf16[8,512,512]{2,1,0:T(8,128)(2,1)} %fusion.69) | data formatting | bytes 8388608 | tf_op jit(solution)/shard_map/stack | solution.py:55
  89.3 8.4 %all-to-all-start = ((bf16[8,512,512]{2,0,1:T(8,128)(2,1)}), bf16[8,512,512]{2,0,1:T(8,128)(2,1)}, u32[]{:S(2)}, u32[]{:S(2)}) async-start(bf16[8,512,512]{2,0,1:T(8,128)(2,1)} %copy.5), calls=%async_computation | async-start | bytes 8388608 | tf_op jit(solution)/shard_map/all_to_all | solution.py:57
  98.0 92.8 %all-to-all-done = bf16[8,512,512]{2,0,1:T(8,128)(2,1)} async-done(((bf16[8,512,512]{2,0,1:T(8,128)(2,1)}), bf16[8,512,512]{2,0,1:T(8,128)(2,1)}, u32[]{:S(2)}, u32[]{:S(2)}) %all-to-all-start) | async-done | bytes 4194336 | tf_op jit(solution)/shard_map/all_to_all | solution.py:57
  197.1 5.6 %convolution_convert_fusion = bf16[128,32768]{1,0:T(8,128)(2,1)} fusion(bf16[64,32768]{1,0:T(8,128)(2,1)S(1)} %bitcast.83, bf16[64,64]{1,0:T(8,128)(2,1)S(1)} %get-tuple-element.12, bf16[64,64]{1,0:T(8,128)(2,1)S(1)} %get-tuple-element.13), kind=kOutput, calls=%fused_computation | convolution fusion | flops 541097984 | bytes 12599296 | tf_op jit(solution)/shard_map/dot_general | solution.py:60
  202.7 13.6 %reshape_reshape.3 = bf16[8192,512]{1,0:T(8,128)(2,1)} reshape(bf16[128,32768]{1,0:T(8,128)(2,1)} %convolution_convert_fusion) | data formatting | bytes 16777216 | tf_op jit(solution)/shard_map/reshape;reshape | solution.py:68
  216.3 10.2 %copy.11 = bf16[16,8,64,512]{3,2,1,0:T(8,128)(2,1)} copy(bf16[16,8,64,512]{3,1,2,0:T(8,128)(2,1)} %bitcast.69) | data formatting | bytes 16777216
  226.6 8.0 %constant_dynamic-update-slice_fusion = bf16[2,64,71,512]{3,2,1,0:T(8,128)(2,1)} fusion(bf16[2,64,64,512]{3,2,1,0:T(8,128)(2,1)} %bitcast.79), kind=kLoop, calls=%fused_computation.94 | loop fusion | bytes 16777216
  237.5 9.1 %fusion.113 = f32[8192,256]{1,0:T(8,128)} fusion(bf16[8192,512]{1,0:T(8,128)(2,1)} %reshape_reshape.3, s32[512,256]{1,0:T(8,128)S(1)} %copy-done), kind=kOutput, calls=%fused_computation.70 | convolution fusion | flops 2147614720 | bytes 17301504 | tf_op jit(solution)/shard_map/dot_general | solution.py:75
  246.7 12.5 %collective-permute-done.1 = bf16[2,64,7,512]{3,1,2,0:T(8,128)(2,1)S(1)} collective-permute-done((bf16[2,64,7,512]{3,1,2,0:T(8,128)(2,1)S(1)}, bf16[2,64,7,512]{3,1,2,0:T(8,128)(2,1)S(1)}, u32[]{:S(2)}, u32[]{:S(2)}) %collective-permute-start.1) | collective-permute-done | bytes 917536 | tf_op jit(solution)/shard_map/ppermute | solution.py:18
  260.7 52.8 %fusion.142 = (bf16[2,64,64,512]{3,2,1,0:T(8,128)(2,1)}, bf16[2,64,64,512]{3,2,1,0:T(8,128)(2,1)}, bf16[2,64,64,512]{3,2,1,0:T(8,128)(2,1)}, bf16[2,64,64,512]{3...) fusion(bf16[2,64,71,512]{3,2,1,0:T(8,128)(2,1)} %copy_dynamic-u, ...), kind=kLoop, calls=%fused_computation.106 | loop fusion | bytes 117440512 | tf_op jit(solution)/shard_map/slice | solution.py:68
  313.6 8.4 %convolution_add_fusion.6 = f32[8192,256]{1,0:T(8,128)S(1)} fusion(f32[8192,256]{1,0:T(8,128)} %fusion.113, bf16[8192,512]{1,0:T(8,128)(2,1)} %bitcast.78, s32[512,256]{1,0:T(8,128)S(1)} %copy-done), kind=kOutput, calls=%fused_computation.8 | convolution fusion | flops 2149711872 | bytes 25690112 | tf_op jit(solution)/shard_map/dot_general | solution.py:75
  322.0 6.1 %convolution_add_fusion.5 = f32[8192,256]{1,0:T(8,128)S(1)} fusion(f32[8192,256]{1,0:T(8,128)S(1)} %convolution_add_fusion.6, bf16[8192,512]{1,0:T(8,128)(2,1)} %bitcast.77, s32[512,256]{1,0:T(8,128)S(1)} %copy-done), kind=kOutput, calls=%fused_computation.7 | convolution fusion | flops 2149711872 | bytes 25690112 | tf_op jit(solution)/shard_map/dot_general | solution.py:75
  328.1 6.1 %convolution_add_fusion.4 = f32[8192,256]{1,0:T(8,128)S(1)} fusion(f32[8192,256]{1,0:T(8,128)S(1)} %convolution_add_fusion.5, bf16[8192,512]{1,0:T(8,128)(2,1)} %bitcast.76, s32[512,256]{1,0:T(8,128)S(1)} %copy-done), kind=kOutput, calls=%fused_computation.6 | convolution fusion | flops 2149711872 | bytes 25690112 | tf_op jit(solution)/shard_map/dot_general | solution.py:75
  336.7 6.3 %convolution_add_fusion.2 = f32[8192,256]{1,0:T(8,128)S(1)} fusion(f32[8192,256]{1,0:T(8,128)S(1)} %convolution_add_fusion.3, bf16[8192,512]{1,0:T(8,128)(2,1)} %bitcast.72, s32[512,256]{1,0:T(8,128)S(1)} %copy-done), kind=kOutput, calls=%fused_computation.4 | convolution fusion | flops 2149711872 | bytes 25690112 | tf_op jit(solution)/shard_map/dot_general | solution.py:75
  343.0 6.0 %convolution_add_fusion.1 = f32[8192,256]{1,0:T(8,128)S(1)} fusion(f32[8192,256]{1,0:T(8,128)S(1)} %convolution_add_fusion.2, bf16[8192,512]{1,0:T(8,128)(2,1)} %bitcast.71, s32[512,256]{1,0:T(8,128)S(1)} %copy-done), kind=kOutput, calls=%fused_computation.3 | convolution fusion | flops 2149711872 | bytes 25690112 | tf_op jit(solution)/shard_map/dot_general | solution.py:75
  349.0 9.2 %fusion = f32[8192,256]{1,0:T(8,128)} fusion(f32[8192,256]{1,0:T(8,128)S(1)} %convolution_add_fusion.1, bf16[8192,512]{1,0:T(8,128)(2,1)} %bitcast.70, s32[512,256]{1,0:T(8,128)S(1)} %copy-done), kind=kOutput, calls=%fused_computation.2 | convolution fusion | flops 2151809024 | bytes 25690112 | tf_op jit(solution)/shard_map/dot_general | solution.py:75
  358.2 39.2 %all-reduce.3.cloned.1.call-done = f32[8192,256]{1,0:T(8,128)} async-done(((f32[8192,256]{1,0:T(8,128)}), f32[8192,256]{1,0:T(8,128)}) %all-reduce.3.cloned.1.call-update) | async-done | bytes 8388624 | tf_op jit(solution)/shard_map/psum | solution.py:78
  (47 shorter events, 38.5 us)
Async XLA Ops:
  7.6 68.9 %collective-permute-start = (bf16[511,512]{1,0:T(8,128)(2,1)S(1)}, bf16[511,512]{1,0:T(8,128)(2,1)S(1)}, u32[]{:S(2)}, u32[]{:S(2)}) collective-permute-start(bf16[511,512]{1,0:T(8,128)(2,1)S(1)} %slice.73), channel_id=1, source_target_pairs={{2,0},{4,2},{6,4},{8,6},{10,8},{12,10},{14,12},{3,1},{5,3},{7,5},{... | collective-permute-start | bytes 1569800 | tf_op jit(solution)/shard_map/ppermute | solution.py:18
  40.9 7.3 %copy-start.1 = (bf16[512,4606]{1,0:T(8,128)(2,1)S(1)}, bf16[512,4606]{1,0:T(8,128)(2,1)}, u32[]{:S(2)}) copy-start(bf16[512,4606]{1,0:T(8,128)(2,1)} %convert_element_type.50) | copy-start | bytes 14149636
  48.2 12.6 %slice-start.2 = ((s8[33546240]{0:T(1024)(128)(4,1)}), s8[4194304]{0:T(1024)(128)(4,1)S(1)}, s32[]{:S(2)}) async-start(s8[33546240]{0:T(1024)(128)(4,1)} %bitcast.81), calls=%async_computation.4 | async-start | bytes 8388608
  48.2 12.6 %slice-start.3 = ((s8[33546240]{0:T(1024)(128)(4,1)}), s8[4194304]{0:T(1024)(128)(4,1)S(1)}, s32[]{:S(2)}) async-start(s8[33546240]{0:T(1024)(128)(4,1)} %bitcast.81), calls=%async_computation.5 | async-start | bytes 8388608
  48.2 12.6 %slice-start.4 = ((s8[33546240]{0:T(1024)(128)(4,1)}), s8[4194304]{0:T(1024)(128)(4,1)S(1)}, s32[]{:S(2)}) async-start(s8[33546240]{0:T(1024)(128)(4,1)} %bitcast.81), calls=%async_computation.6 | async-start | bytes 8388608
  48.3 12.6 %slice-start.5 = ((s8[33546240]{0:T(1024)(128)(4,1)}), s8[4194304]{0:T(1024)(128)(4,1)S(1)}, s32[]{:S(2)}) async-start(s8[33546240]{0:T(1024)(128)(4,1)} %bitcast.81), calls=%async_computation.7 | async-start | bytes 8388608
  48.3 12.6 %slice-start.6 = ((s8[33546240]{0:T(1024)(128)(4,1)}), s8[4194304]{0:T(1024)(128)(4,1)S(1)}, s32[]{:S(2)}) async-start(s8[33546240]{0:T(1024)(128)(4,1)} %bitcast.81), calls=%async_computation.8 | async-start | bytes 8388608
  54.2 6.6 %slice-start.7 = ((s8[33546240]{0:T(1024)(128)(4,1)}), s8[4194304]{0:T(1024)(128)(4,1)S(1)}, s32[]{:S(2)}) async-start(s8[33546240]{0:T(1024)(128)(4,1)} %bitcast.81), calls=%async_computation.9 | async-start | bytes 8388608
  54.2 6.7 %slice-start.8 = ((s8[33546240]{0:T(1024)(128)(4,1)}), s8[4194304]{0:T(1024)(128)(4,1)S(1)}, s32[]{:S(2)}) async-start(s8[33546240]{0:T(1024)(128)(4,1)} %bitcast.81), calls=%async_computation.10 | async-start | bytes 8388608
  54.2 8.0 %slice-start.9 = ((s8[33546240]{0:T(1024)(128)(4,1)}), s8[4186112]{0:T(1024)(128)(4,1)S(1)}, s32[]{:S(2)}) async-start(s8[33546240]{0:T(1024)(128)(4,1)} %bitcast.81), calls=%async_computation.11 | async-start | bytes 8372224
  89.3 101.4 %all-to-all-start = ((bf16[8,512,512]{2,0,1:T(8,128)(2,1)}), bf16[8,512,512]{2,0,1:T(8,128)(2,1)}, u32[]{:S(2)}, u32[]{:S(2)}) async-start(bf16[8,512,512]{2,0,1:T(8,128)(2,1)} %copy.5), calls=%async_computation | async-start | bytes 8388608 | tf_op jit(solution)/shard_map/all_to_all | solution.py:57
  97.8 299.7 %all-reduce.3.cloned.1.call-start = ((), (), s32[]{:S(2)}) async-start(), calls=%async_computation.1 | async-start | bytes 16777216 | tf_op jit(solution)/shard_map/psum | solution.py:78
  226.6 10.9 %copy-start = (s32[512,256]{1,0:T(8,128)S(1)}, s32[512,256]{1,0:T(8,128)}, u32[]{:S(2)}) copy-start(s32[512,256]{1,0:T(8,128)} %param.5) | copy-start | bytes 1572868
  236.2 22.9 %collective-permute-start.1 = (bf16[2,64,7,512]{3,1,2,0:T(8,128)(2,1)S(1)}, bf16[2,64,7,512]{3,1,2,0:T(8,128)(2,1)S(1)}, u32[]{:S(2)}, u32[]{:S(2)}) collective-permute-start(bf16[2,64,7,512]{3,1,2,0:T(8,128)(2,1)S(1)} %copy.9), channel_id=1, source_target_pairs={{2,0},{4,2},{6,4},{8,6},{10,8},{12,10},{14,12},{3,1},{5,3},{7,5},{... | collective-permute-start | bytes 2752520 | tf_op jit(solution)/shard_map/ppermute | solution.py:18
  322.0 12.3 %slice-start = ((s8[8388608]{0:T(1024)(128)(4,1)}), s8[4194304]{0:T(1024)(128)(4,1)S(1)}, s32[]{:S(2)}) async-start(s8[8388608]{0:T(1024)(128)(4,1)} %bitcast.73), calls=%async_computation.2 | async-start | bytes 8388608
  328.1 6.2 %slice-start.1 = ((s8[8388608]{0:T(1024)(128)(4,1)}), s8[4194304]{0:T(1024)(128)(4,1)S(1)}, s32[]{:S(2)}) async-start(s8[8388608]{0:T(1024)(128)(4,1)} %bitcast.73), calls=%async_computation.3 | async-start | bytes 8388608
Sparse Core Ops, SparseCore 0:
  358.3 39.0 all-reduce.2
where the time goes:
time: 416 us; the launch traced here: 409 us
  waiting for transfers between devices  145 us (35%)
  local copies, waits for them, and re-layouts  135 us (32%)
  matrix products  99.3 us (24%)
  between operations  14.1 us (3%)
  starting transfers between devices  11 us (3%)
  other arithmetic  4.64 us (1%)
    all_to_all x1, waiting for transfers between devices, body(): lax.all_to_all(profiles, 'tm', split_axis=1, concat_axis=0, tiled=True)  92.8 us
    dot_general x8, matrix products, body(): jnp.dot(shifted_list[offset], selector, preferred_element_type=jnp.float32)  53.7 us
    slice x1, local copies, waits for them, and re-layouts, body(): spec_ext[:, :, offset:offset + delay_rows, :]  52.8 us
    dot_general x8, matrix products, body(): jnp.dot(toeplitz, segment, preferred_element_type=jnp.float32) * norm_code  40 us
    psum x1, waiting for transfers between devices, body(): summed = lax.psum(partial_sum * norm_hydro, 'hyd')  39.2 us
    unnamed x28, local copies, waits for them, and re-layouts  22.6 us
    another operation x2, local copies, waits for them, and re-layouts, toeplitz_code(): tiled = jnp.tile(padded, DELAYS)[:DELAYS * seg_len]  14.3 us
    another operation x1, local copies, waits for them, and re-layouts, body(): spec_ext[:, :, offset:offset + delay_rows, :]  13.6 us
  transfers between devices with their start and end apart: 4, of which 3 were waited for; matrix products, arithmetic and copies ran while one was open for 18% of the time, Pallas kernels for 0%

commit v1 on v0

--- a/solution.py
+++ b/solution.py
@@ -10,6 +10,30 @@
 PERIODS = 64
 BEAMS = 256
 MAXLAG = 8
+
+
+def cut_along(array, dim, size):
+    shape = array.shape
+    blocks = array.reshape(*shape[:dim], size, shape[dim] // size, *shape[dim + 1 :])
+    return jnp.moveaxis(blocks, dim, 0)
+
+
+def in_order(blocks, dim):
+    lengths = list(blocks.shape[1:])
+    lengths[dim] *= blocks.shape[0]
+    return jnp.moveaxis(blocks, 0, dim).reshape(lengths)
+
+
+def exchange_directly(shard, axis, split_dim, concat_dim):
+    size, here = (lax.axis_size(axis), lax.axis_index(axis))
+    blocks = cut_along(shard, split_dim, size)
+    out = blocks
+    for lap in range(1, size):
+        target, source = ((here + lap) % size, (here - lap) % size)
+        sent = lax.dynamic_index_in_dim(blocks, target, 0)
+        other = lax.ppermute(sent, axis, [(i, (i + lap) % size) for i in range(size)])
+        out = lax.dynamic_update_slice_in_dim(out, other, source, axis=0)
+    return in_order(out, concat_dim)
 
 
 def passed_along(array, axis, by):
@@ -54,7 +78,7 @@
         )
     profiles = jnp.stack(profile_list, 0)
     transform = dft_table(PERIODS)
-    received = lax.all_to_all(profiles, "tm", split_axis=1, concat_axis=0, tiled=True)
+    received = exchange_directly(profiles, "tm", 1, 0)
     trailing = received.shape[1:]
     flattened = received.reshape(received.shape[0], -1)
     spectral = jnp.dot(transform, flattened, preferred_element_type=jnp.float32).astype(

time: 416 us -> 421 us (1.012)
  waiting for transfers between devices: 145 us -> 117 us
  local copies, waits for them, and re-layouts: 135 us -> 154 us
  starting transfers between devices: 11 us -> 26.3 us
    all_to_all x1 -> x0, waiting for transfers between devices: 92.8 us -> none  [body(): lax.all_to_all(profiles, 'tm', split_axis=1, concat_axis=0, tiled=True)]
    ppermute x0 -> x7, waiting for transfers between devices: none -> 38.6 us  [exchange_directly(): lax.ppermute(sent, axis, [(i, (i + lap) % size) for i in range(size)])]
    ppermute x0 -> x7, starting transfers between devices: none -> 23.3 us  [exchange_directly(): lax.ppermute(sent, axis, [(i, (i + lap) % size) for i in range(size)])]
    psum x1, waiting for transfers between devices: 39.2 us -> 58.6 us  [body(): summed = lax.psum(partial_sum * norm_hydro, 'hyd')]
    unnamed x28 -> x35, local copies, waits for them, and re-layouts: 22.6 us -> 37 us
    dynamic_update_slice x0 -> x7, local copies, waits for them, and re-layouts: none -> 11.2 us  [exchange_directly(): out = lax.dynamic_update_slice_in_dim(out, other, source, axis=0)]
    all_to_all x1 -> x0, starting transfers between devices: 8.43 us -> none  [body(): lax.all_to_all(profiles, 'tm', split_axis=1, concat_axis=0, tiled=True)]
    ppermute x2, waiting for transfers between devices: 12.5 us -> 19.6 us  [passed_along(): return lax.ppermute(array, axis, pairs)]
  transfers between devices with their start and end apart: 4 -> 10, of which waited for: 3 -> 5; matrix products, arithmetic and copies ran while one was open for 18% -> 23% of each run, Pallas kernels for 0% -> 0%
where the time goes in v1:
time: 421 us; the launch traced here: 414 us
  local copies, waits for them, and re-layouts  154 us (37%)
  waiting for transfers between devices  117 us (28%)
  matrix products  98.3 us (23%)
  starting transfers between devices  26.3 us (6%)
  between operations  14 us (3%)
  other arithmetic  4.63 us (1%)
    psum x1, waiting for transfers between devices, body(): summed = lax.psum(partial_sum * norm_hydro, 'hyd')  58.6 us
    dot_general x8, matrix products, body(): jnp.dot(shifted_list[offset], selector, preferred_element_type=jnp.float32)  53.6 us
    slice x1, local copies, waits for them, and re-layouts, body(): spec_ext[:, :, offset:offset + delay_rows, :]  52.8 us
    dot_general x8, matrix products, body(): jnp.dot(toeplitz, segment, preferred_element_type=jnp.float32) * norm_code  39.1 us
    ppermute x7, waiting for transfers between devices, exchange_directly(): lax.ppermute(sent, axis, [(i, (i + lap) % size) for i in range(size)])  38.6 us
    unnamed x35, local copies, waits for them, and re-layouts  37 us
    ppermute x7, starting transfers between devices, exchange_directly(): lax.ppermute(sent, axis, [(i, (i + lap) % size) for i in range(size)])  23.3 us
    ppermute x2, waiting for transfers between devices, passed_along(): return lax.ppermute(array, axis, pairs)  19.6 us
  transfers between devices with their start and end apart: 10, of which 5 were waited for; matrix products, arithmetic and copies ran while one was open for 23% of the time, Pallas kernels for 0%

profile of v1, /device:TPU:0, one launch (start us, length us, event | category | flops | bytes accessed | tf_op | source)
XLA Modules:
  0.0 413.8 jit_solution(959727972618772256)
XLA Ops:
  12.2 11.8 %tile.11 = bf16[2358784]{0:T(1024)(128)(2,1)} reshape(bf16[512,4607]{1,0:T(8,128)(2,1)} %tile.10) | data formatting | bytes 9435136 | tf_op jit(solution)/shard_map/tile | solution.py:48
  23.9 5.9 %slice.85 = bf16[2358272]{0:T(1024)(128)(2,1)} slice(bf16[2358784]{0:T(1024)(128)(2,1)} %tile.11), slice={[0:2358272]} | slice | bytes 9433088 | tf_op jit(solution)/shard_map/slice | solution.py:48
  29.9 11.3 %convert_element_type.50 = bf16[512,4606]{1,0:T(8,128)(2,1)} reshape(bf16[2358272]{0:T(1024)(128)(2,1)} %slice.85) | data formatting | bytes 9433088 | tf_op jit(solution)/shard_map/convert_element_type | solution.py:49
  41.2 7.3 %fusion.59 = bf16[512,512]{1,0:T(8,128)(2,1)} fusion(bf16[512,4606]{1,0:T(8,128)(2,1)} %convert_element_type.50, bf16[32760,512]{1,0:T(8,128)(2,1)} %param.3), kind=kOutput, calls=%fused_computation.44 | convolution fusion | flops 2415394816 | bytes 9961472 | tf_op jit(solution)/shard_map/dot_general | solution.py:75
  48.5 5.9 %fusion.55 = bf16[512,512]{1,0:T(8,128)(2,1)} fusion(bf16[512,4606]{1,0:T(8,128)(2,1)S(1)} %copy-done.1, bf16[32760,512]{1,0:T(8,128)(2,1)} %param.3), kind=kOutput, calls=%fused_computation.42 | convolution fusion | flops 2415394816 | bytes 9959424 | tf_op jit(solution)/shard_map/dot_general | solution.py:75
  54.5 6.6 %fusion.52 = bf16[512,512]{1,0:T(8,128)(2,1)} fusion(bf16[512,4606]{1,0:T(8,128)(2,1)S(1)} %copy-done.1, bf16[32760,512]{1,0:T(8,128)(2,1)} %param.3), kind=kOutput, calls=%fused_computation.41 | convolution fusion | flops 2415394816 | bytes 9959424 | tf_op jit(solution)/shard_map/dot_general | solution.py:75
  87.9 6.3 %fusion.58 = bf16[512,512]{1,0:T(8,128)(2,1)S(1)} fusion(bf16[512,4606]{1,0:T(8,128)(2,1)} %convert_element_type.50, bf16[511,512]{1,0:T(8,128)(2,1)S(1)} %collective-permute-done, bf16[32760,512]{1,0:T(8,128)(2,1)} %param.3), kind=kOutput, calls=%fused_computation.43 | convolution fusion | flops 2424827904 | bytes 39310336 | tf_op jit(solution)/shard_map/dot_general | solution.py:75
  110.7 7.9 %collective-permute-done.1 = bf16[1,8,64,512]{3,2,1,0:T(8,128)(2,1)} collective-permute-done((bf16[1,8,64,512]{3,2,1,0:T(8,128)(2,1)}, bf16[1,8,64,512]{3,2,1,0:T(8,128)(2,1)}, u32[]{:S(2)}, u32[]{:S(2)}) %collective-permute-start.1) | collective-permute-done | bytes 524320 | tf_op jit(solution)/shard_map/ppermute | solution.py:34
  123.2 8.3 %collective-permute-start.7 = (bf16[1,8,64,512]{3,2,1,0:T(8,128)(2,1)S(1)}, bf16[1,8,64,512]{3,2,1,0:T(8,128)(2,1)S(1)}, u32[]{:S(2)}, u32[]{:S(2)}) collective-permute-start(bf16[1,8,64,512]{3,2,1,0:T(8,128)(2,1)S(1)} %get-tuple-element.12), channel_id=1, source_target_pairs={{0,14},{2,0},{4,2},{6,4},{8,6},{10,8},{12,10},{14,12},{1,15},{3,1}... | collective-permute-start | bytes 1572872 | tf_op jit(solution)/shard_map/ppermute | solution.py:34
  133.5 28.9 %collective-permute-done.3 = bf16[1,8,64,512]{3,2,1,0:T(8,128)(2,1)} collective-permute-done((bf16[1,8,64,512]{3,2,1,0:T(8,128)(2,1)S(1)}, bf16[1,8,64,512]{3,2,1,0:T(8,128)(2,1)}, u32[]{:S(2)}, u32[]{:S(2)}) %collective-permute-start.3) | collective-permute-done | bytes 524320 | tf_op jit(solution)/shard_map/ppermute | solution.py:34
  176.2 5.6 %convolution_convert_fusion = bf16[128,32768]{1,0:T(8,128)(2,1)} fusion(bf16[64,32768]{1,0:T(8,128)(2,1)S(1)} %bitcast.86, bf16[64,64]{1,0:T(8,128)(2,1)S(1)} %get-tuple-element.19, bf16[64,64]{1,0:T(8,128)(2,1)S(1)} %get-tuple-element.20), kind=kOutput, calls=%fused_computation | convolution fusion | flops 541097984 | bytes 12599296 | tf_op jit(solution)/shard_map/dot_general | solution.py:84
  181.8 13.5 %reshape_reshape.7 = bf16[8192,512]{1,0:T(8,128)(2,1)} reshape(bf16[128,32768]{1,0:T(8,128)(2,1)} %convolution_convert_fusion) | data formatting | bytes 16777216 | tf_op jit(solution)/shard_map/reshape;reshape | solution.py:92
  195.3 10.3 %copy.24 = bf16[16,8,64,512]{3,2,1,0:T(8,128)(2,1)} copy(bf16[16,8,64,512]{3,1,2,0:T(8,128)(2,1)} %bitcast.72) | data formatting | bytes 16777216
  205.5 7.9 %constant_dynamic-update-slice_fusion.8 = bf16[2,64,71,512]{3,2,1,0:T(8,128)(2,1)} fusion(bf16[2,64,64,512]{3,2,1,0:T(8,128)(2,1)} %bitcast.82), kind=kLoop, calls=%fused_computation.92 | loop fusion | bytes 16777216
  216.8 9.1 %fusion.69 = f32[8192,256]{1,0:T(8,128)} fusion(bf16[8192,512]{1,0:T(8,128)(2,1)} %reshape_reshape.7, s32[512,256]{1,0:T(8,128)S(1)} %copy-done), kind=kOutput, calls=%fused_computation.60 | convolution fusion | flops 2147614720 | bytes 17301504 | tf_op jit(solution)/shard_map/dot_general | solution.py:99
  225.9 19.6 %collective-permute-done.8 = bf16[2,64,7,512]{3,1,2,0:T(8,128)(2,1)S(1)} collective-permute-done((bf16[2,64,7,512]{3,1,2,0:T(8,128)(2,1)S(1)}, bf16[2,64,7,512]{3,1,2,0:T(8,128)(2,1)S(1)}, u32[]{:S(2)}, u32[]{:S(2)}) %collective-permute-start.8) | collective-permute-done | bytes 917536 | tf_op jit(solution)/shard_map/ppermute | solution.py:42
  247.0 52.8 %fusion.98 = (bf16[2,64,64,512]{3,2,1,0:T(8,128)(2,1)}, bf16[2,64,64,512]{3,2,1,0:T(8,128)(2,1)}, bf16[2,64,64,512]{3,2,1,0:T(8,128)(2,1)}, bf16[2,64,64,512]{3,...) fusion(bf16[2,64,71,512]{3,2,1,0:T(8,128)(2,1)} %copy_dynamic-u, ...), kind=kLoop, calls=%fused_computation.111 | loop fusion | bytes 117440512 | tf_op jit(solution)/shard_map/slice | solution.py:92
  299.8 8.4 %convolution_add_fusion.6 = f32[8192,256]{1,0:T(8,128)S(1)} fusion(f32[8192,256]{1,0:T(8,128)} %fusion.69, bf16[8192,512]{1,0:T(8,128)(2,1)} %bitcast.81, s32[512,256]{1,0:T(8,128)S(1)} %copy-done), kind=kOutput, calls=%fused_computation.8 | convolution fusion | flops 2149711872 | bytes 25690112 | tf_op jit(solution)/shard_map/dot_general | solution.py:99
  308.2 6.1 %convolution_add_fusion.5 = f32[8192,256]{1,0:T(8,128)S(1)} fusion(f32[8192,256]{1,0:T(8,128)S(1)} %convolution_add_fusion.6, bf16[8192,512]{1,0:T(8,128)(2,1)} %bitcast.80, s32[512,256]{1,0:T(8,128)S(1)} %copy-done), kind=kOutput, calls=%fused_computation.7 | convolution fusion | flops 2149711872 | bytes 25690112 | tf_op jit(solution)/shard_map/dot_general | solution.py:99
  314.4 6.1 %convolution_add_fusion.4 = f32[8192,256]{1,0:T(8,128)S(1)} fusion(f32[8192,256]{1,0:T(8,128)S(1)} %convolution_add_fusion.5, bf16[8192,512]{1,0:T(8,128)(2,1)} %bitcast.79, s32[512,256]{1,0:T(8,128)S(1)} %copy-done), kind=kOutput, calls=%fused_computation.6 | convolution fusion | flops 2149711872 | bytes 25690112 | tf_op jit(solution)/shard_map/dot_general | solution.py:99
  323.0 6.2 %convolution_add_fusion.2 = f32[8192,256]{1,0:T(8,128)S(1)} fusion(f32[8192,256]{1,0:T(8,128)S(1)} %convolution_add_fusion.3, bf16[8192,512]{1,0:T(8,128)(2,1)} %bitcast.75, s32[512,256]{1,0:T(8,128)S(1)} %copy-done), kind=kOutput, calls=%fused_computation.4 | convolution fusion | flops 2149711872 | bytes 25690112 | tf_op jit(solution)/shard_map/dot_general | solution.py:99
  329.2 6.0 %convolution_add_fusion.1 = f32[8192,256]{1,0:T(8,128)S(1)} fusion(f32[8192,256]{1,0:T(8,128)S(1)} %convolution_add_fusion.2, bf16[8192,512]{1,0:T(8,128)(2,1)} %bitcast.74, s32[512,256]{1,0:T(8,128)S(1)} %copy-done), kind=kOutput, calls=%fused_computation.3 | convolution fusion | flops 2149711872 | bytes 25690112 | tf_op jit(solution)/shard_map/dot_general | solution.py:99
  335.2 9.1 %fusion = f32[8192,256]{1,0:T(8,128)} fusion(f32[8192,256]{1,0:T(8,128)S(1)} %convolution_add_fusion.1, bf16[8192,512]{1,0:T(8,128)(2,1)} %bitcast.73, s32[512,256]{1,0:T(8,128)S(1)} %copy-done), kind=kOutput, calls=%fused_computation.2 | convolution fusion | flops 2151809024 | bytes 25690112 | tf_op jit(solution)/shard_map/dot_general | solution.py:99
  344.4 58.6 %all-reduce.3.cloned.1.call-done = f32[8192,256]{1,0:T(8,128)} async-done(((f32[8192,256]{1,0:T(8,128)}), f32[8192,256]{1,0:T(8,128)}) %all-reduce.3.cloned.1.call-update) | async-done | bytes 8388624 | tf_op jit(solution)/shard_map/psum | solution.py:102
  (73 shorter events, 80.3 us)
Async XLA Ops:
  6.5 396.4 %all-reduce.3.cloned.1.call-start = ((), (), s32[]{:S(2)}) async-start(), calls=%async_computation | async-start | bytes 16777216 | tf_op jit(solution)/shard_map/psum | solution.py:102
  7.6 80.3 %collective-permute-start = (bf16[511,512]{1,0:T(8,128)(2,1)S(1)}, bf16[511,512]{1,0:T(8,128)(2,1)S(1)}, u32[]{:S(2)}, u32[]{:S(2)}) collective-permute-start(bf16[511,512]{1,0:T(8,128)(2,1)S(1)} %slice.73), channel_id=1, source_target_pairs={{2,0},{4,2},{6,4},{8,6},{10,8},{12,10},{14,12},{3,1},{5,3},{7,5},{... | collective-permute-start | bytes 1569800 | tf_op jit(solution)/shard_map/ppermute | solution.py:42
  41.2 7.3 %copy-start.1 = (bf16[512,4606]{1,0:T(8,128)(2,1)S(1)}, bf16[512,4606]{1,0:T(8,128)(2,1)}, u32[]{:S(2)}) copy-start(bf16[512,4606]{1,0:T(8,128)(2,1)} %convert_element_type.50) | copy-start | bytes 14149636
  48.5 12.6 %slice-start.2 = ((s8[33546240]{0:T(1024)(128)(4,1)}), s8[4194304]{0:T(1024)(128)(4,1)S(1)}, s32[]{:S(2)}) async-start(s8[33546240]{0:T(1024)(128)(4,1)} %bitcast.84), calls=%async_computation.3 | async-start | bytes 8388608
  48.5 12.6 %slice-start.3 = ((s8[33546240]{0:T(1024)(128)(4,1)}), s8[4194304]{0:T(1024)(128)(4,1)S(1)}, s32[]{:S(2)}) async-start(s8[33546240]{0:T(1024)(128)(4,1)} %bitcast.84), calls=%async_computation.4 | async-start | bytes 8388608
  48.5 12.6 %slice-start.4 = ((s8[33546240]{0:T(1024)(128)(4,1)}), s8[4194304]{0:T(1024)(128)(4,1)S(1)}, s32[]{:S(2)}) async-start(s8[33546240]{0:T(1024)(128)(4,1)} %bitcast.84), calls=%async_computation.5 | async-start | bytes 8388608
  48.5 12.6 %slice-start.5 = ((s8[33546240]{0:T(1024)(128)(4,1)}), s8[4194304]{0:T(1024)(128)(4,1)S(1)}, s32[]{:S(2)}) async-start(s8[33546240]{0:T(1024)(128)(4,1)} %bitcast.84), calls=%async_computation.6 | async-start | bytes 8388608
  48.5 12.6 %slice-start.6 = ((s8[33546240]{0:T(1024)(128)(4,1)}), s8[4194304]{0:T(1024)(128)(4,1)S(1)}, s32[]{:S(2)}) async-start(s8[33546240]{0:T(1024)(128)(4,1)} %bitcast.84), calls=%async_computation.7 | async-start | bytes 8388608
  54.5 6.6 %slice-start.7 = ((s8[33546240]{0:T(1024)(128)(4,1)}), s8[4194304]{0:T(1024)(128)(4,1)S(1)}, s32[]{:S(2)}) async-start(s8[33546240]{0:T(1024)(128)(4,1)} %bitcast.84), calls=%async_computation.8 | async-start | bytes 8388608
  54.5 6.7 %slice-start.8 = ((s8[33546240]{0:T(1024)(128)(4,1)}), s8[4194304]{0:T(1024)(128)(4,1)S(1)}, s32[]{:S(2)}) async-start(s8[33546240]{0:T(1024)(128)(4,1)} %bitcast.84), calls=%async_computation.9 | async-start | bytes 8388608
  54.5 8.1 %slice-start.9 = ((s8[33546240]{0:T(1024)(128)(4,1)}), s8[4186112]{0:T(1024)(128)(4,1)S(1)}, s32[]{:S(2)}) async-start(s8[33546240]{0:T(1024)(128)(4,1)} %bitcast.84), calls=%async_computation.10 | async-start | bytes 8372224
  98.1 20.4 %collective-permute-start.1 = (bf16[1,8,64,512]{3,2,1,0:T(8,128)(2,1)}, bf16[1,8,64,512]{3,2,1,0:T(8,128)(2,1)}, u32[]{:S(2)}, u32[]{:S(2)}) collective-permute-start(bf16[1,8,64,512]{3,2,1,0:T(8,128)(2,1)} %get-tuple-element.18), channel_id=1, source_target_pairs={{0,2},{2,4},{4,6},{6,8},{8,10},{10,12},{12,14},{14,0},{1,3},{3,5},... | collective-permute-start | bytes 1572872 | tf_op jit(solution)/shard_map/ppermute | solution.py:34
  101.7 21.5 %collective-permute-start.2 = (bf16[1,8,64,512]{3,2,1,0:T(8,128)(2,1)S(1)}, bf16[1,8,64,512]{3,2,1,0:T(8,128)(2,1)}, u32[]{:S(2)}, u32[]{:S(2)}) collective-permute-start(bf16[1,8,64,512]{3,2,1,0:T(8,128)(2,1)S(1)} %get-tuple-element.17), channel_id=1, source_target_pairs={{0,4},{2,6},{4,8},{6,10},{8,12},{10,14},{12,0},{14,2},{1,5},{3,7},... | collective-permute-start | bytes 1572872 | tf_op jit(solution)/shard_map/ppermute | solution.py:34
  103.8 58.5 %collective-permute-start.3 = (bf16[1,8,64,512]{3,2,1,0:T(8,128)(2,1)S(1)}, bf16[1,8,64,512]{3,2,1,0:T(8,128)(2,1)}, u32[]{:S(2)}, u32[]{:S(2)}) collective-permute-start(bf16[1,8,64,512]{3,2,1,0:T(8,128)(2,1)S(1)} %get-tuple-element.16), channel_id=1, source_target_pairs={{0,6},{2,8},{4,10},{6,12},{8,14},{10,0},{12,2},{14,4},{1,7},{3,9},... | collective-permute-start | bytes 1572872 | tf_op jit(solution)/shard_map/ppermute | solution.py:34
  107.4 56.8 %collective-permute-start.4 = (bf16[1,8,64,512]{3,2,1,0:T(8,128)(2,1)S(1)}, bf16[1,8,64,512]{3,2,1,0:T(8,128)(2,1)}, u32[]{:S(2)}, u32[]{:S(2)}) collective-permute-start(bf16[1,8,64,512]{3,2,1,0:T(8,128)(2,1)S(1)} %get-tuple-element.15), channel_id=1, source_target_pairs={{0,8},{2,10},{4,12},{6,14},{8,0},{10,2},{12,4},{14,6},{1,9},{3,11}... | collective-permute-start | bytes 1572872 | tf_op jit(solution)/shard_map/ppermute | solution.py:34
  108.7 57.4 %collective-permute-start.5 = (bf16[1,8,64,512]{3,2,1,0:T(8,128)(2,1)S(1)}, bf16[1,8,64,512]{3,2,1,0:T(8,128)(2,1)}, u32[]{:S(2)}, u32[]{:S(2)}) collective-permute-start(bf16[1,8,64,512]{3,2,1,0:T(8,128)(2,1)S(1)} %get-tuple-element.14), channel_id=1, source_target_pairs={{0,10},{2,12},{4,14},{6,0},{8,2},{10,4},{12,6},{14,8},{1,11},{3,13... | collective-permute-start | bytes 1572872 | tf_op jit(solution)/shard_map/ppermute | solution.py:34
  118.6 49.4 %collective-permute-start.6 = (bf16[1,8,64,512]{3,2,1,0:T(8,128)(2,1)S(1)}, bf16[1,8,64,512]{3,2,1,0:T(8,128)(2,1)S(1)}, u32[]{:S(2)}, u32[]{:S(2)}) collective-permute-start(bf16[1,8,64,512]{3,2,1,0:T(8,128)(2,1)S(1)} %get-tuple-element.13), channel_id=1, source_target_pairs={{0,12},{2,14},{4,0},{6,2},{8,4},{10,6},{12,8},{14,10},{1,13},{3,15... | collective-permute-start | bytes 1572872 | tf_op jit(solution)/shard_map/ppermute | solution.py:34
  123.2 47.4 %collective-permute-start.7 = (bf16[1,8,64,512]{3,2,1,0:T(8,128)(2,1)S(1)}, bf16[1,8,64,512]{3,2,1,0:T(8,128)(2,1)S(1)}, u32[]{:S(2)}, u32[]{:S(2)}) collective-permute-start(bf16[1,8,64,512]{3,2,1,0:T(8,128)(2,1)S(1)} %get-tuple-element.12), channel_id=1, source_target_pairs={{0,14},{2,0},{4,2},{6,4},{8,6},{10,8},{12,10},{14,12},{1,15},{3,1}... | collective-permute-start | bytes 1572872 | tf_op jit(solution)/shard_map/ppermute | solution.py:34
  205.5 11.2 %copy-start = (s32[512,256]{1,0:T(8,128)S(1)}, s32[512,256]{1,0:T(8,128)}, u32[]{:S(2)}) copy-start(s32[512,256]{1,0:T(8,128)} %param.5) | copy-start | bytes 1572868
  215.1 30.4 %collective-permute-start.8 = (bf16[2,64,7,512]{3,1,2,0:T(8,128)(2,1)S(1)}, bf16[2,64,7,512]{3,1,2,0:T(8,128)(2,1)S(1)}, u32[]{:S(2)}, u32[]{:S(2)}) collective-permute-start(bf16[2,64,7,512]{3,1,2,0:T(8,128)(2,1)S(1)} %copy.22), channel_id=1, source_target_pairs={{2,0},{4,2},{6,4},{8,6},{10,8},{12,10},{14,12},{3,1},{5,3},{7,5},{... | collective-permute-start | bytes 2752520 | tf_op jit(solution)/shard_map/ppermute | solution.py:42
  308.2 12.3 %slice-start = ((s8[8388608]{0:T(1024)(128)(4,1)}), s8[4194304]{0:T(1024)(128)(4,1)S(1)}, s32[]{:S(2)}) async-start(s8[8388608]{0:T(1024)(128)(4,1)} %bitcast.76), calls=%async_computation.1 | async-start | bytes 8388608
  314.4 6.2 %slice-start.1 = ((s8[8388608]{0:T(1024)(128)(4,1)}), s8[4194304]{0:T(1024)(128)(4,1)S(1)}, s32[]{:S(2)}) async-start(s8[8388608]{0:T(1024)(128)(4,1)} %bitcast.76), calls=%async_computation.2 | async-start | bytes 8388608
Sparse Core Ops, SparseCore 0:
  344.5 58.4 all-reduce.2
